TPU v7x, 32 devices: a whole 2x2x4 slice. The times are simulated.
32 devices in a mesh: shot: 16 (over z, y, core), tm: 2 (over x).
Axes of the slice: x: 2, y: 2, z: 4, core: 2. Of those that a mesh axis runs over, the one named last changes fastest.
Arguments:
- records: bfloat16 [16, 4, 32, 256], P('shot', None, None, 'tm'), may hold values from -6 to 6
- fan_taps: bfloat16 [4, 15, 15], replicated, may hold values from -0.29882812 to 0.29882812
- dip_taps: bfloat16 [15, 15], replicated, may hold values from -0.29882812 to 0.29882812
- live_mask: int32 [16, 32], P('shot'), may hold values from 0 to 1, as said below
- node_place: int32 [32], replicated, may hold values from 0 to 31, as said below
- shot_place: int32 [16], replicated, may hold values from 0 to 15, as said below
Outputs:
- node_gathers: bfloat16 [16, 4, 32, 256], P(None, None, 'shot', 'tm')
Inputs may be any that keep to these rules, and one draw needn't show every extreme that they name: `live_mask`: A trace is live only where the node lies within 16 positions of the shot's point on the receiver line; some traces inside that band are dead too. `node_place`: A permutation: every position once. `shot_place`: A permutation: every position once.
All inputs are finite; a program needn't handle non-finite values.
Results may differ from a plain program's by a relative error of at most 0.0049.
Values may be sent and summed in bfloat16 or wider, within the bound.
A program may use at most 64 MiB of HBM per device.

v0:
```python
import jax
import jax.numpy as jnp
from jax import lax
from jax.sharding import PartitionSpec as P


def with_halo(block, sides, width):
    for axis, dim in sides:
        count = lax.axis_size(axis)
        forward = [(i, i + 1) for i in range(count - 1)]
        backward = [(target, source) for source, target in forward]
        low = lax.ppermute(
            lax.slice_in_dim(block, block.shape[dim] - width, None, axis=dim), axis, forward
        )
        high = lax.ppermute(lax.slice_in_dim(block, 0, width, axis=dim), axis, backward)
        block = jnp.concatenate([low, block, high], axis=dim)
    return block


def tap_tables(tap_set, out_width):
    tap_count = tap_set.shape[1]
    extent = out_width + tap_count - 1
    row_iota = lax.broadcasted_iota(jnp.int32, (extent, out_width, tap_count), 0)
    col_iota = lax.broadcasted_iota(jnp.int32, (extent, out_width, tap_count), 1)
    tap_iota = lax.broadcasted_iota(jnp.int32, (extent, out_width, tap_count), 2)
    onehot = (row_iota - col_iota == tap_iota).astype(jnp.bfloat16)
    tables = jnp.einsum(
        "gab,jtb->gjat", tap_set, onehot, preferred_element_type=jnp.float32
    ).astype(jnp.bfloat16)
    return tables.reshape(tap_set.shape[0], extent, tap_count * out_width)


def shifted_total(products, along, tap_count, out_width):
    tap_reach = (tap_count - 1) // 2
    length = products.shape[along]
    split = products.reshape(products.shape[:-1] + (tap_count, out_width))
    widths = [(0, 0)] * split.ndim
    widths[along] = (tap_reach, tap_reach)
    padded = jnp.pad(split, widths)
    total = lax.slice_in_dim(padded, 0, length, axis=along)[..., 0, :]
    for offset in range(1, tap_count):
        total = (
            total + lax.slice_in_dim(padded, offset, offset + length, axis=along)[..., offset, :]
        )
    return total


def on_device(records, fan_taps, dip_taps, live_mask, node_place, shot_place):
    samples = records.shape[3]
    tap_count = fan_taps.shape[1]
    tap_reach = (tap_count - 1) // 2
    node_order = jnp.argsort(node_place)
    shot_order = jnp.argsort(shot_place)
    extended = with_halo(records, (("tm", 3),), tap_reach)
    ordered = jnp.take(extended, node_order, axis=2)
    fan_table = tap_tables(fan_taps, samples)
    fan_products = jnp.einsum(
        "scnj,cjk->scnk", ordered, fan_table, preferred_element_type=jnp.float32
    )
    fan_field = shifted_total(fan_products, 2, tap_count, samples)
    keep_mask = jnp.take(live_mask, node_order, axis=1).astype(jnp.float32)[:, None, :, None]
    fanned = (fan_field * keep_mask).astype(jnp.bfloat16)
    dip_table = tap_tables(dip_taps[None], samples)[0]
    arranged = jnp.take(
        lax.all_to_all(fanned, "shot", split_axis=2, concat_axis=0, tiled=True), shot_order, axis=0
    )
    widened = with_halo(arranged, (("tm", 3),), tap_reach)
    dip_products = jnp.dot(widened, dip_table, preferred_element_type=jnp.float32)
    result = shifted_total(dip_products, 0, tap_count, samples)
    return result.astype(jnp.bfloat16)


def solution(mesh):
    return jax.shard_map(
        on_device,
        mesh=mesh,
        in_specs=(P("shot", None, None, "tm"), P(), P(), P("shot", None), P(), P()),
        out_specs=P(None, None, "shot", "tm"),
        check_vma=False,
    )
```

profile of v0, /device:TPU:0, one launch (start us, length us, event | category | flops | bytes accessed | tf_op | source)
XLA Modules:
  0.0 45.5 jit_solution(17676757350754263001)
XLA Ops:
  0.0 0.8 %copy.22 = bf16[1,4,32,128]{3,1,2,0:T(4,128)(2,1)S(1)} copy(bf16[1,4,32,128]{3,2,1,0:T(8,128)(2,1)} %param.6) | data formatting | bytes 65536 | tf_op args[0]
  0.8 0.1 fusion.46
  0.9 4.8 %collective-permute-start = (bf16[1,4,32,7]{3,1,2,0:T(4,128)(2,1)S(1)}, bf16[1,4,32,7]{3,1,2,0:T(4,128)(2,1)S(1)}, u32[]{:S(2)}, u32[]{:S(2)}) collective-permute-start(bf16[1,4,32,7]{3,1,2,0:T(4,128)(2,1)S(1)} %get-tuple-element.13), channel_id=1, source_target_pairs={{0,1},{2,3},{4,5},{6,7},{8,9},{10,11},{12,13},{14,15},{16,17},{18,... | collective-permute-start | bytes 5384 | tf_op jit(solution)/shard_map/ppermute | solution.py:12
  5.8 1.3 %collective-permute-start.1 = (bf16[1,4,32,7]{3,1,2,0:T(4,128)(2,1)S(1)}, bf16[1,4,32,7]{3,1,2,0:T(4,128)(2,1)S(1)}, u32[]{:S(2)}, u32[]{:S(2)}) collective-permute-start(bf16[1,4,32,7]{3,1,2,0:T(4,128)(2,1)S(1)} %get-tuple-element.14), channel_id=1, source_target_pairs={{1,0},{3,2},{5,4},{7,6},{9,8},{11,10},{13,12},{15,14},{17,16},{19,... | collective-permute-start | bytes 5384 | tf_op jit(solution)/shard_map/ppermute | solution.py:15
  7.1 2.3 %sort.35 = (s32[32]{0:T(128)}, s32[32]{0:T(128)S(1)}) sort(s32[32]{0:T(128)} %param.10, s32[32]{0:T(128)S(1)} %iota.39), dimensions={0}, to_apply=%region_1.2 | sort | flops 160 | bytes 512 | tf_op jit(solution)/shard_map/jit(argsort)/sort | solution.py:52
  9.3 1.4 %gather_fusion.1 = s32[32]{0:T(128)S(1)} fusion(s32[32]{0:T(128)} %bitcast.52, s32[1024]{0:T(1024)S(1)} %pad_clamp_fusion.1), kind=kCustom, calls=%fused_computation.1 | custom fusion | bytes 384 | tf_op jit(solution)/shard_map/jit(_take)/gather | solution.py:61
  10.7 1.5 %convert_bitcast_fusion = bf16[4,142,15,128]{3,2,0,1:T(8,128)(2,1)S(1)} fusion(bf16[4,15,15]{2,0,1:T(4,128)(2,1)} %param.7), kind=kOutput, calls=%fused_computation.32 | convolution fusion | flops 34352640 | bytes 2182920 | tf_op jit(solution)/shard_map/gab,jtb->gjat/dot_general | solution.py:27
  12.2 1.2 %sort.34 = (s32[16]{0:T(128)}, s32[16]{0:T(128)S(1)}) sort(s32[16]{0:T(128)S(1)} %copy-done.1, s32[16]{0:T(128)S(1)} %iota.35), dimensions={0}, to_apply=%region_0.0 | sort | flops 64 | bytes 256 | tf_op jit(solution)/shard_map/jit(argsort)/sort | solution.py:53
  13.5 2.8 %reshape.295 = bf16[4,142,1920]{2,0,1:T(4,128)(2,1)} reshape(bf16[4,142,15,128]{3,2,0,1:T(8,128)(2,1)S(1)} %convert_bitcast_fusion) | data formatting | bytes 4362240 | tf_op jit(solution)/shard_map/reshape | solution.py:30
  16.3 0.1 maximum_bitcast_fusion
  16.4 0.6 %gather_fusion = bf16[32,4,142]{2,1,0:T(4,128)(2,1)S(1)} fusion(bf16[4,32,142]{2,0,1:T(4,128)(2,1)S(1)} %maximum_bitcast_fusion, s32[1024]{0:T(1024)S(1)} %pad_clamp_fusion.1), kind=kCustom, calls=%fused_computation | custom fusion | bytes 72832 | tf_op jit(solution)/shard_map/jit(_take)/gather | solution.py:55
  17.0 0.1 select_bitcast_fusion
  17.1 2.0 %convolution_bitcast_fusion = f32[1,4,32,1920]{3,2,1,0:T(8,128)S(1)} fusion(bf16[4,142,1920]{2,0,1:T(4,128)(2,1)} %reshape.295, bf16[4,32,142]{2,0,1:T(4,128)(2,1)S(1)} %select_bitcast_fusion), kind=kOutput, calls=%fused_computation.31 | convolution fusion | flops 69795840 | bytes 3200512 | tf_op jit(solution)/shard_map/scnj,cjk->scnk/dot_general | solution.py:57
  19.2 0.2 reshape.235
  19.4 0.6 %fusion.18 = f32[1,4,32,1,128]{4,3,2,1,0:T(1,128)S(1)} fusion(f32[1,4,32,15,128]{4,3,2,1,0:T(8,128)S(1)} %reshape.235), kind=kLoop, calls=%fused_computation.52 | loop fusion | flops 229376 | bytes 1179648 | tf_op jit(solution)/shard_map/add | solution.py:43
  20.0 0.1 multiply_convert_fusion
  20.1 0.6 %copy.26 = bf16[1,4,32,128]{3,1,0,2:T(4,128)(2,1)} copy(bf16[1,4,32,128]{3,2,1,0:T(8,128)(2,1)S(1)} %multiply_convert_fusion) | data formatting | bytes 65536 | tf_op jit(solution)/shard_map/convert_element_type | solution.py:62
  20.7 5.9 %all-to-all-start = ((bf16[1,4,32,128]{3,1,0,2:T(4,128)(2,1)}), bf16[1,4,32,128]{3,1,0,2:T(4,128)(2,1)S(1)}, u32[]{:S(2)}, u32[]{:S(2)}) async-start(bf16[1,4,32,128]{3,1,0,2:T(4,128)(2,1)} %copy.26), calls=%async_computation | async-start | bytes 65536 | tf_op jit(solution)/shard_map/all_to_all | solution.py:65
  26.7 6.6 %all-to-all-done = bf16[1,4,32,128]{3,1,0,2:T(4,128)(2,1)S(1)} async-done(((bf16[1,4,32,128]{3,1,0,2:T(4,128)(2,1)}), bf16[1,4,32,128]{3,1,0,2:T(4,128)(2,1)S(1)}, u32[]{:S(2)}, u32[]{:S(2)}) %all-to-all-start) | async-done | bytes 32800 | tf_op jit(solution)/shard_map/all_to_all | solution.py:65
  33.3 0.6 %gather_fusion.2 = bf16[16,4,2,128]{3,1,2,0:T(4,128)(2,1)S(1)} fusion(bf16[16,4,2,128]{3,1,2,0:T(4,128)(2,1)S(1)} %bitcast.57, s32[1024]{0:T(1024)S(1)} %pad_clamp_fusion), kind=kCustom, calls=%fused_computation.2 | custom fusion | bytes 65600 | tf_op jit(solution)/shard_map/jit(_take)/gather | solution.py:64
  33.9 0.1 copy_select_fusion
  34.0 0.1 fusion.45
  34.0 4.5 %collective-permute-start.2 = (bf16[16,4,2,7]{3,0,2,1:T(8,128)(2,1)S(1)}, bf16[16,4,2,7]{3,0,2,1:T(8,128)(2,1)S(1)}, u32[]{:S(2)}, u32[]{:S(2)}) collective-permute-start(bf16[16,4,2,7]{3,0,2,1:T(8,128)(2,1)S(1)} %get-tuple-element.11), channel_id=1, source_target_pairs={{0,1},{2,3},{4,5},{6,7},{8,9},{10,11},{12,13},{14,15},{16,17},{18,... | collective-permute-start | bytes 5384 | tf_op jit(solution)/shard_map/ppermute | solution.py:12
  38.6 1.3 %collective-permute-start.3 = (bf16[16,4,2,7]{3,0,2,1:T(8,128)(2,1)S(1)}, bf16[16,4,2,7]{3,0,2,1:T(8,128)(2,1)S(1)}, u32[]{:S(2)}, u32[]{:S(2)}) collective-permute-start(bf16[16,4,2,7]{3,0,2,1:T(8,128)(2,1)S(1)} %get-tuple-element.12), channel_id=1, source_target_pairs={{1,0},{3,2},{5,4},{7,6},{9,8},{11,10},{13,12},{15,14},{17,16},{19,... | collective-permute-start | bytes 5384 | tf_op jit(solution)/shard_map/ppermute | solution.py:15
  39.9 0.4 fusion.1
  40.3 0.1 pad.19
  40.4 0.2 copy.36
  40.6 0.4 dot_general.23
  41.0 3.4 %collective-permute-done.3 = bf16[16,4,2,7]{3,0,2,1:T(8,128)(2,1)S(1)} collective-permute-done((bf16[16,4,2,7]{3,0,2,1:T(8,128)(2,1)S(1)}, bf16[16,4,2,7]{3,0,2,1:T(8,128)(2,1)S(1)}, u32[]{:S(2)}, u32[]{:S(2)}) %collective-permute-start.3) | collective-permute-done | bytes 1824 | tf_op jit(solution)/shard_map/ppermute | solution.py:15
  44.4 0.3 fusion.4
  44.7 0.1 fusion.40
  44.9 0.6 %copy.29 = bf16[16,4,2,128]{3,2,1,0:T(2,128)(2,1)} copy(bf16[16,4,2,128]{3,0,2,1:T(8,128)(2,1)S(1)} %fusion.40) | data formatting | bytes 65536 | tf_op jit(solution)/shard_map/convert_element_type | solution.py:70
  (15 shorter events, 0.1 us)
Async XLA Ops:
  0.0 39.9 %copy-start = (bf16[15,15]{1,0:T(8,128)(2,1)S(1)}, bf16[15,15]{1,0:T(8,128)(2,1)}, u32[]{:S(2)}) copy-start(bf16[15,15]{1,0:T(8,128)(2,1)} %param.8) | copy-start | bytes 1354
  0.8 11.4 %copy-start.1 = (s32[16]{0:T(128)S(1)}, s32[16]{0:T(128)}, u32[]{:S(2)}) copy-start(s32[16]{0:T(128)} %param.11) | copy-start | bytes 196
  0.9 15.4 %collective-permute-start = (bf16[1,4,32,7]{3,1,2,0:T(4,128)(2,1)S(1)}, bf16[1,4,32,7]{3,1,2,0:T(4,128)(2,1)S(1)}, u32[]{:S(2)}, u32[]{:S(2)}) collective-permute-start(bf16[1,4,32,7]{3,1,2,0:T(4,128)(2,1)S(1)} %get-tuple-element.13), channel_id=1, source_target_pairs={{0,1},{2,3},{4,5},{6,7},{8,9},{10,11},{12,13},{14,15},{16,17},{18,... | collective-permute-start | bytes 5384 | tf_op jit(solution)/shard_map/ppermute | solution.py:12
  5.8 10.5 %collective-permute-start.1 = (bf16[1,4,32,7]{3,1,2,0:T(4,128)(2,1)S(1)}, bf16[1,4,32,7]{3,1,2,0:T(4,128)(2,1)S(1)}, u32[]{:S(2)}, u32[]{:S(2)}) collective-permute-start(bf16[1,4,32,7]{3,1,2,0:T(4,128)(2,1)S(1)} %get-tuple-element.14), channel_id=1, source_target_pairs={{1,0},{3,2},{5,4},{7,6},{9,8},{11,10},{13,12},{15,14},{17,16},{19,... | collective-permute-start | bytes 5384 | tf_op jit(solution)/shard_map/ppermute | solution.py:15
  20.7 12.6 %all-to-all-start = ((bf16[1,4,32,128]{3,1,0,2:T(4,128)(2,1)}), bf16[1,4,32,128]{3,1,0,2:T(4,128)(2,1)S(1)}, u32[]{:S(2)}, u32[]{:S(2)}) async-start(bf16[1,4,32,128]{3,1,0,2:T(4,128)(2,1)} %copy.26), calls=%async_computation | async-start | bytes 65536 | tf_op jit(solution)/shard_map/all_to_all | solution.py:65
  34.0 7.0 %collective-permute-start.2 = (bf16[16,4,2,7]{3,0,2,1:T(8,128)(2,1)S(1)}, bf16[16,4,2,7]{3,0,2,1:T(8,128)(2,1)S(1)}, u32[]{:S(2)}, u32[]{:S(2)}) collective-permute-start(bf16[16,4,2,7]{3,0,2,1:T(8,128)(2,1)S(1)} %get-tuple-element.11), channel_id=1, source_target_pairs={{0,1},{2,3},{4,5},{6,7},{8,9},{10,11},{12,13},{14,15},{16,17},{18,... | collective-permute-start | bytes 5384 | tf_op jit(solution)/shard_map/ppermute | solution.py:12
  38.6 5.8 %collective-permute-start.3 = (bf16[16,4,2,7]{3,0,2,1:T(8,128)(2,1)S(1)}, bf16[16,4,2,7]{3,0,2,1:T(8,128)(2,1)S(1)}, u32[]{:S(2)}, u32[]{:S(2)}) collective-permute-start(bf16[16,4,2,7]{3,0,2,1:T(8,128)(2,1)S(1)} %get-tuple-element.12), channel_id=1, source_target_pairs={{1,0},{3,2},{5,4},{7,6},{9,8},{11,10},{13,12},{15,14},{17,16},{19,... | collective-permute-start | bytes 5384 | tf_op jit(solution)/shard_map/ppermute | solution.py:15
where the time goes:
time: 45.9 us; the launch traced here: 45.5 us
  starting transfers between devices  17.9 us (39%)
  waiting for transfers between devices  9.98 us (22%)
  local copies, waits for them, and re-layouts  8.54 us (19%)
  other arithmetic  4.64 us (10%)
  matrix products  4.26 us (9%)
    ppermute x2, starting transfers between devices, with_halo(): lax.ppermute(lax.slice_in_dim(block, block.shape[dim] - width, None, axis...  9.38 us
    all_to_all x1, waiting for transfers between devices, on_device(): lax.all_to_all(fanned, 'shot', split_axis=2, concat_axis=0, tiled=True)  6.62 us
    all_to_all x1, starting transfers between devices, on_device(): lax.all_to_all(fanned, 'shot', split_axis=2, concat_axis=0, tiled=True)  5.94 us
    ppermute x2, waiting for transfers between devices, with_halo(): lax.ppermute(lax.slice_in_dim(block, 0, width, axis=dim), axis, backward)  3.35 us
    reshape x1, local copies, waits for them, and re-layouts, tap_tables(): return tables.reshape(tap_set.shape[0], extent, tap_count * out_width)  2.82 us
    ppermute x2, starting transfers between devices, with_halo(): lax.ppermute(lax.slice_in_dim(block, 0, width, axis=dim), axis, backward)  2.58 us
    sort x1, other arithmetic, on_device(): node_order = jnp.argsort(node_place)  2.26 us
    dot_general x1, matrix products, on_device(): jnp.einsum('scnj,cjk->scnk', ordered, fan_table, preferred_element_type=j...  2.04 us
  transfers between devices with their start and end apart: 5, of which 2 were waited for; matrix products, arithmetic and copies ran while one was open for 23% of the time, Pallas kernels for 0%

commit v1 on v0

v1 whole, which is shorter than its diff:
```python
import functools

import jax
import jax.numpy as jnp
from jax import lax
from jax.experimental import pallas as pl
from jax.experimental.pallas import tpu as pltpu
from jax.sharding import PartitionSpec as P

MESH = pl.DeviceIdType.MESH


def repeat(count, body):
    if count <= 32:
        for step in range(count):
            body(step)
    else:
        lax.fori_loop(0, count, lambda step, carry: (body(step), carry)[1], 0)


def spread_taps(taps, groups, width):
    first = lax.broadcasted_iota(jnp.int32, (taps.shape[1], width), 0) * groups
    lane = lax.broadcasted_iota(jnp.int32, (taps.shape[1], width), 1)
    onehot = jnp.where((lane >= first) & (lane < first + groups), 1.0, 0.0).astype(jnp.bfloat16)
    return jnp.dot(taps, onehot, preferred_element_type=jnp.float32)


def spread_places(place, groups, width):
    row = lax.broadcasted_iota(jnp.int32, (groups, width), 0)
    lane = lax.broadcasted_iota(jnp.int32, (groups, width), 1)
    onehot = jnp.where(lax.rem(lane, groups) == row, 1.0, 0.0).astype(jnp.bfloat16)
    left = jnp.broadcast_to(place.astype(jnp.float32), (8, groups)).astype(jnp.bfloat16)
    return jnp.dot(left, onehot, preferred_element_type=jnp.float32).astype(jnp.int32)


def kernel(
    records_ref, fan_ref, dip_ref, live_ref, node_ref, shot_ref, out_ref,
    traces, matrix, shifted, framed, send, recv, flat, rows, pack, from_low, from_high,
    load_sem, send_sem, recv_sem, pack_sem, low_sem, high_sem,
):
    comps, nodes, samples = traces.shape
    devices = send.shape[0]
    each = nodes // devices
    groups = comps * each
    tap_count = dip_ref.shape[0]
    reach = (tap_count - 1) // 2
    me, win = lax.axis_index("shot"), lax.axis_index("tm")
    windows = lax.axis_size("tm")
    has_low, has_high = win > 0, win < windows - 1

    load = pltpu.make_async_copy(records_ref.at[0], traces, load_sem)
    load.start()

    barrier = pltpu.get_barrier_semaphore()

    def greet(step):
        pl.semaphore_signal(
            barrier, inc=1, device_id=(lax.rem(me + step + 1, devices), win), device_id_type=MESH
        )

    repeat(devices - 1, greet)
    for there, side in ((has_low, -1), (has_high, 1)):
        @pl.when(there)
        def _():
            repeat(devices, lambda step: pl.semaphore_signal(
                barrier, inc=1, device_id=(lax.rem(me + step, devices), win + side),
                device_id_type=MESH,
            ))

    depth = matrix.shape[2]
    taps = [spread_taps(fan_ref[c], nodes, depth) for c in range(comps)]
    places = spread_places(node_ref[...], nodes, depth)[0:1]
    block = min(devices, 16)

    def build(step):
        for j in range(each):
            at = (lax.broadcasted_iota(jnp.int32, (block, depth), 0) + step * block) * each + j
            apart = places - at + reach
            sums = [jnp.zeros((block, depth), jnp.float32)] * comps
            for a in range(tap_count):
                hit = apart == a
                sums = [jnp.where(hit, taps[c][a : a + 1], sums[c]) for c in range(comps)]
            for c in range(comps):
                start = j * devices + step * block
                if not isinstance(step, int):
                    start = pl.multiple_of(start, block)
                matrix[c, pl.ds(start, block), :] = sums[c].astype(jnp.bfloat16)

    if devices == block:
        build(0)
    else:
        lax.fori_loop(0, devices // block, lambda step, carry: (build(step), carry)[1], 0)

    position = lax.broadcasted_iota(jnp.int32, (devices, nodes), 0) * each
    alive = []
    for j in range(each):
        here = node_ref[...] == position + j
        kept = jnp.where(here, live_ref[...].astype(jnp.float32), 0.0)
        alive.append(jnp.sum(kept, axis=1, keepdims=True))

    load.wait()
    lane = lax.broadcasted_iota(jnp.int32, (nodes, samples), 1)
    for c in range(comps):
        trace = traces[c].astype(jnp.float32)
        for b in range(tap_count):
            move = b - reach
            turned = pltpu.roll(trace, (-move) % samples, 1) if move else trace
            inside = (lane < samples - move) if move >= 0 else (lane >= -move)
            shifted[c, b * nodes : (b + 1) * nodes, :samples] = (
                jnp.where(inside, turned, 0.0).astype(jnp.bfloat16)
            )
            shifted[c, b * nodes : (b + 1) * nodes, samples:] = (
                jnp.where(inside, 0.0, turned).astype(jnp.bfloat16)
            )
        rest = depth - tap_count * nodes
        shifted[c, tap_count * nodes :, :] = jnp.zeros((rest, 2 * samples), jnp.bfloat16)

    lane = lax.broadcasted_iota(jnp.int32, (devices, samples), 1)
    stride = samples // groups
    to_low = jnp.zeros((devices, samples), jnp.float32)
    to_high = jnp.zeros((devices, samples), jnp.float32)
    for c in range(comps):
        field = jnp.dot(matrix[c], shifted[c], preferred_element_type=jnp.float32)
        for j in range(each):
            g = c * each + j
            part = field[j * devices : (j + 1) * devices] * alive[j]
            inner, outer = part[:, :samples], part[:, samples:]
            flat[pl.ds(g, devices, stride=2 * groups), :] = inner
            flat[pl.ds(groups + g, devices, stride=2 * groups), :] = outer
            mine = (lane >= g * stride) & (lane < g * stride + 2 * reach)
            turn = (reach + g * stride) % samples
            low = jnp.where(lane >= samples // 2, outer, inner)
            high = jnp.where(lane >= samples // 2, inner, outer)
            to_low = jnp.where(mine, pltpu.roll(low, turn, 1), to_low)
            to_high = jnp.where(mine, pltpu.roll(high, turn, 1), to_high)
    send[...] = flat[...].astype(jnp.bfloat16).reshape(send.shape)
    pack[0] = to_low[:, None, :]
    pack[1] = to_high[:, None, :]

    pl.semaphore_wait(
        barrier,
        devices - 1 + devices * (jnp.where(has_low, 1, 0) + jnp.where(has_high, 1, 0)),
    )

    def post(step):
        target = lax.rem(me + step + 1, devices)
        pltpu.make_async_remote_copy(
            src_ref=send.at[target], dst_ref=recv.at[me], send_sem=send_sem, recv_sem=recv_sem,
            device_id=(target, win), device_id_type=MESH,
        ).start()

    repeat(devices - 1, post)
    sides = (
        (has_low, -1, 0, from_high, high_sem),
        (has_high, 1, 1, from_low, low_sem),
    )
    for there, side, slot, landing, landed in sides:
        @pl.when(there)
        def _():
            def post_side(step):
                target = lax.rem(me + step, devices)
                pltpu.make_async_remote_copy(
                    src_ref=pack.at[slot, target], dst_ref=landing.at[me],
                    send_sem=pack_sem.at[slot], recv_sem=landed,
                    device_id=(target, win + side), device_id_type=MESH,
                ).start()

            repeat(devices, post_side)

    recv[me] = send[me]

    span = framed.shape[0]
    dips = spread_taps(dip_ref[...], devices, span)
    apart = (
        spread_places(shot_ref[...], devices, span)[0:1]
        - lax.broadcasted_iota(jnp.int32, (devices, span), 0) + reach
    )
    dip = jnp.zeros((devices, span), jnp.float32)
    for a in range(tap_count):
        dip = jnp.where(apart == a, dips[a : a + 1], dip)
    dip = dip.astype(jnp.bfloat16)

    for there, landing, landed in ((has_high, from_high, high_sem), (has_low, from_low, low_sem)):
        @pl.when(there)
        def _():
            pltpu.make_async_copy(landing, landing, landed).wait()

        @pl.when(jnp.logical_not(there))
        def _():
            landing[...] = jnp.zeros(landing.shape, jnp.float32)

    others = recv.at[pl.ds(0, devices - 1)]
    pltpu.make_async_copy(others, others, recv_sem).wait()

    rows[...] = recv[...].reshape(rows.shape).astype(jnp.float32)
    high_edge = from_high[...].reshape(devices, samples)
    low_edge = from_low[...].reshape(devices, samples)
    head, tail = lane < reach, lane >= samples - reach
    keep = (head & has_high) | (tail & has_low)
    for g in range(groups):
        turn = (samples - reach - g * stride) % samples
        high = pltpu.roll(high_edge, turn, 1)
        low = pltpu.roll(low_edge, turn, 1)
        inner = rows[pl.ds(g, devices, stride=2 * groups), :]
        outer = rows[pl.ds(groups + g, devices, stride=2 * groups), :]
        inner = inner + jnp.where(tail, high, jnp.where(head, low, 0.0))
        outer = jnp.where(keep, outer + jnp.where(head, high, low), 0.0)
        columns = slice(g * samples, (g + 1) * samples)
        for b in range(tap_count):
            move = b - reach
            if move > 0:
                both = jnp.where(lane < move, outer, inner)
            else:
                both = jnp.where(lane >= samples + move, outer, inner)
            turned = pltpu.roll(both, (-move) % samples, 1) if move else inner
            framed[b * devices : (b + 1) * devices, columns] = turned.astype(jnp.bfloat16)
    rest = span - tap_count * devices
    framed[tap_count * devices :, :] = jnp.zeros((rest, groups * samples), jnp.bfloat16)
    out_ref[...] = jnp.dot(dip, framed[...], preferred_element_type=jnp.float32).astype(jnp.bfloat16)

    sent = send.at[pl.ds(0, devices - 1)]
    pltpu.make_async_copy(sent, sent, send_sem).wait()
    for there, slot in ((has_low, 0), (has_high, 1)):
        @pl.when(there)
        def _():
            pltpu.make_async_copy(pack.at[slot], pack.at[slot], pack_sem.at[slot]).wait()


def on_device(devices, records, fan_taps, dip_taps, live_mask, node_place, shot_place):
    _, comps, nodes, samples = records.shape
    each = nodes // devices
    groups = comps * each
    slots = fan_taps.shape[1] + 1
    vmem = pl.BlockSpec(memory_space=pltpu.VMEM)
    result = pl.pallas_call(
        kernel,
        out_shape=jax.ShapeDtypeStruct((devices, groups * samples), jnp.bfloat16),
        in_specs=[pl.BlockSpec(memory_space=pl.ANY)] + [vmem] * 5,
        out_specs=vmem,
        scratch_shapes=[
            pltpu.VMEM((comps, nodes, samples), jnp.bfloat16),
            pltpu.VMEM((comps, nodes, slots * nodes), jnp.bfloat16),
            pltpu.VMEM((comps, slots * nodes, 2 * samples), jnp.bfloat16),
            pltpu.VMEM((slots * devices, groups * samples), jnp.bfloat16),
            pltpu.VMEM((devices, 2 * groups, samples), jnp.bfloat16),
            pltpu.VMEM((devices, 2 * groups, samples), jnp.bfloat16),
            pltpu.VMEM((devices * 2 * groups, samples), jnp.float32),
            pltpu.VMEM((devices * 2 * groups, samples), jnp.float32),
            pltpu.VMEM((2, devices, 1, samples), jnp.float32),
            pltpu.VMEM((devices, 1, samples), jnp.float32),
            pltpu.VMEM((devices, 1, samples), jnp.float32),
            pltpu.SemaphoreType.DMA,
            pltpu.SemaphoreType.DMA,
            pltpu.SemaphoreType.DMA,
            pltpu.SemaphoreType.DMA((2,)),
            pltpu.SemaphoreType.DMA,
            pltpu.SemaphoreType.DMA,
        ],
        compiler_params=pltpu.CompilerParams(
            collective_id=0, has_side_effects=True, vmem_limit_bytes=48 * 1024 * 1024
        ),
    )(records, fan_taps, dip_taps, live_mask, node_place[None], shot_place[None])
    return result.reshape(devices, comps, each, samples)


def solution(mesh):
    return jax.shard_map(
        functools.partial(on_device, mesh.shape["shot"]),
        mesh=mesh,
        in_specs=(P("shot", None, None, "tm"), P(), P(), P("shot", None), P(), P()),
        out_specs=P(None, None, "shot", "tm"),
        check_vma=False,
    )
```

time: 45.9 us -> 13.2 us (0.29)
  starting transfers between devices: 17.9 us -> 0 us
  Pallas kernels: 0 us -> 10.8 us
  waiting for transfers between devices: 9.98 us -> 0 us
  local copies, waits for them, and re-layouts: 8.54 us -> 2.1 us
  other arithmetic: 4.64 us -> 0 us
  matrix products: 4.26 us -> 0 us
    ppermute x4 -> x0, starting transfers between devices: 12 us -> none  [the longest x2 9.38 us: with_halo(): lax.ppermute(lax.slice_in_dim(block, block.shape[dim] - width, None, axis...]
    pallas_call x0 -> x1, Pallas kernels: none -> 10.8 us  [on_device(): pl.pallas_call(kernel, out_shape=jax.ShapeDtypeStruct((devices, groups *...]
    all_to_all x1 -> x0, waiting for transfers between devices: 6.62 us -> none  [on_device(): lax.all_to_all(fanned, 'shot', split_axis=2, concat_axis=0, tiled=True)]
    all_to_all x1 -> x0, starting transfers between devices: 5.94 us -> none  [on_device(): lax.all_to_all(fanned, 'shot', split_axis=2, concat_axis=0, tiled=True)]
    dot_general x4 -> x0, matrix products: 4.26 us -> none  [the longest x1 2.04 us: on_device(): jnp.einsum('scnj,cjk->scnk', ordered, fan_table, preferred_element_type=j...]
    sort x2 -> x0, other arithmetic: 3.5 us -> none  [the longest x1 2.26 us: on_device(): node_order = jnp.argsort(node_place)]
    ppermute x4 -> x0, waiting for transfers between devices: 3.36 us -> none  [the longest x2 3.35 us: with_halo(): lax.ppermute(lax.slice_in_dim(block, 0, width, axis=dim), axis, backward)]
    gather x3 -> x0, local copies, waits for them, and re-layouts: 2.57 us -> none  [the longest x1 1.35 us: on_device(): jnp.take(live_mask, node_order, axis=1).astype(jnp.float32)]
  transfers between devices with their start and end apart: 5 -> 0, of which waited for: 2 -> 0; matrix products, arithmetic and copies ran while one was open for 23% -> 0% of each run, Pallas kernels for 0% -> 0%
where the time goes in v1:
time: 13.2 us; the launch traced here: 12.9 us
  Pallas kernels  10.8 us (82%)
  local copies, waits for them, and re-layouts  2.1 us (16%)
    pallas_call x1, Pallas kernels, on_device(): pl.pallas_call(kernel, out_shape=jax.ShapeDtypeStruct((devices, groups *...  10.8 us
    unnamed x11, local copies, waits for them, and re-layouts  1.47 us
    reshape x1, local copies, waits for them, and re-layouts, on_device(): return result.reshape(devices, comps, each, samples)  0.63 us

profile of v1, /device:TPU:0, one launch (start us, length us, event | category | flops | bytes accessed | tf_op | source)
XLA Modules:
  0.0 12.9 jit_solution(14793640454326209529)
XLA Ops:
  0.0 0.0 copy-start
  0.0 0.0 copy-start.2
  0.0 0.0 copy-start.3
  0.0 0.0 copy-start.4
  0.0 0.8 %copy.7.fan_ref = bf16[4,15,15]{2,1,0:T(8,128)(2,1)S(1)} copy(bf16[4,15,15]{2,0,1:T(4,128)(2,1)} %param.7) | data formatting | bytes 3600 | tf_op args[1]
  0.8 0.0 copy-done
  0.8 0.0 copy-done.2
  0.8 0.0 copy-done.3
  0.8 0.0 copy-done.4
  0.8 0.0 copy-start.1
  0.8 0.7 %copy-done.1 = bf16[15,15]{1,0:T(8,128)(2,1)S(1)} copy-done((bf16[15,15]{1,0:T(8,128)(2,1)S(1)}, bf16[15,15]{1,0:T(8,128)(2,1)}, u32[]{:S(2)}) %copy-start.1) | copy-done | bytes 474
  1.5 10.8 %shard_map.64 = bf16[16,1024]{1,0:T(8,128)(2,1)S(1)} custom-call(bf16[1,4,32,128]{3,2,1,0:T(8,128)(2,1)S(1)} %copy-done, bf16[4,15,15]{2,1,0:T(8,128)(2,1)S(1)} %copy.7.fan_ref, bf16[15,15]{1,0:T(8,128)(2,1)S(1)} %copy-done.1, s32[1,32]{1,0:T(1,128)S(1)} %copy-done.2, s32[1,32]{1,0:T(1,128)S(1)} %bitcast.2, s32[1,16]{1,0:T(1,128)S(1)} %bitcast.3), custom_call_target="tpu_custom_call" | custom-call | tf_op jit(solution)/shard_map/pallas_call | solution.py:235
  12.3 0.6 %reshape.3 = bf16[16,4,2,128]{3,2,1,0:T(2,128)(2,1)} reshape(bf16[16,1024]{1,0:T(8,128)(2,1)S(1)} %shard_map.64) | data formatting | bytes 65536 | tf_op jit(solution)/shard_map/reshape | solution.py:263
Async XLA Ops:
  0.0 0.8 %copy-start = (bf16[1,4,32,128]{3,2,1,0:T(8,128)(2,1)S(1)}, bf16[1,4,32,128]{3,2,1,0:T(8,128)(2,1)}, u32[]{:S(2)}) copy-start(bf16[1,4,32,128]{3,2,1,0:T(8,128)(2,1)} %records_ref.1) | copy-start | bytes 98308
  0.0 0.8 %copy-start.2 = (s32[1,32]{1,0:T(1,128)S(1)}, s32[1,32]{1,0:T(1,128)}, u32[]{:S(2)}) copy-start(s32[1,32]{1,0:T(1,128)} %live_ref.1) | copy-start | bytes 388
  0.0 0.8 %copy-start.3 = (s32[32]{0:T(128)S(1)}, s32[32]{0:T(128)}, u32[]{:S(2)}) copy-start(s32[32]{0:T(128)} %param.10) | copy-start | bytes 388
  0.0 0.8 %copy-start.4 = (s32[16]{0:T(128)S(1)}, s32[16]{0:T(128)}, u32[]{:S(2)}) copy-start(s32[16]{0:T(128)} %param.11) | copy-start | bytes 196
  0.8 0.7 %copy-start.1 = (bf16[15,15]{1,0:T(8,128)(2,1)S(1)}, bf16[15,15]{1,0:T(8,128)(2,1)}, u32[]{:S(2)}) copy-start(bf16[15,15]{1,0:T(8,128)(2,1)} %dip_ref.1) | copy-start | bytes 1354

commit v2 on v1

--- a/solution.py
+++ b/solution.py
@@ -34,8 +34,8 @@
 
 
 def kernel(
-    records_ref, fan_ref, dip_ref, live_ref, node_ref, shot_ref, out_ref,
-    traces, matrix, shifted, framed, send, recv, flat, rows, pack, from_low, from_high,
+    records_src, fan_src, dip_src, live_src, node_src, shot_src, out_ref,
+    traces, fan_ref, dip_ref, live_ref, node_ref, shot_ref, matrix, shifted, framed, send, recv, flat, rows, pack, from_low, from_high,
     load_sem, send_sem, recv_sem, pack_sem, low_sem, high_sem,
 ):
     comps, nodes, samples = traces.shape
@@ -48,8 +48,15 @@
     windows = lax.axis_size("tm")
     has_low, has_high = win > 0, win < windows - 1
 
-    load = pltpu.make_async_copy(records_ref.at[0], traces, load_sem)
-    load.start()
+    loads = [
+        pltpu.make_async_copy(source, held, load_sem.at[i])
+        for i, (source, held) in enumerate((
+            (node_src, node_ref), (fan_src, fan_ref), (records_src.at[0], traces),
+            (live_src, live_ref), (dip_src, dip_ref), (shot_src, shot_ref),
+        ))
+    ]
+    for load in loads:
+        load.start()
 
     barrier = pltpu.get_barrier_semaphore()
 
@@ -68,7 +75,10 @@
             ))
 
     depth = matrix.shape[2]
-    taps = [spread_taps(fan_ref[c], nodes, depth) for c in range(comps)]
+    loads[0].wait()
+    loads[1].wait()
+    tap_rows = fan_ref[...].astype(jnp.float32).reshape(tap_count * comps, tap_count)
+    taps = spread_taps(tap_rows.astype(jnp.bfloat16), nodes, depth)
     places = spread_places(node_ref[...], nodes, depth)[0:1]
     block = min(devices, 16)
 
@@ -79,7 +89,7 @@
             sums = [jnp.zeros((block, depth), jnp.float32)] * comps
             for a in range(tap_count):
                 hit = apart == a
-                sums = [jnp.where(hit, taps[c][a : a + 1], sums[c]) for c in range(comps)]
+                sums = [jnp.where(hit, taps[a * comps + c : a * comps + c + 1], sums[c]) for c in range(comps)]
             for c in range(comps):
                 start = j * devices + step * block
                 if not isinstance(step, int):
@@ -91,6 +101,7 @@
     else:
         lax.fori_loop(0, devices // block, lambda step, carry: (build(step), carry)[1], 0)
 
+    loads[3].wait()
     position = lax.broadcasted_iota(jnp.int32, (devices, nodes), 0) * each
     alive = []
     for j in range(each):
@@ -98,7 +109,7 @@
         kept = jnp.where(here, live_ref[...].astype(jnp.float32), 0.0)
         alive.append(jnp.sum(kept, axis=1, keepdims=True))
 
-    load.wait()
+    loads[2].wait()
     lane = lax.broadcasted_iota(jnp.int32, (nodes, samples), 1)
     for c in range(comps):
         trace = traces[c].astype(jnp.float32)
@@ -169,6 +180,8 @@
 
     recv[me] = send[me]
 
+    loads[4].wait()
+    loads[5].wait()
     span = framed.shape[0]
     dips = spread_taps(dip_ref[...], devices, span)
     apart = (
@@ -235,10 +248,15 @@
     result = pl.pallas_call(
         kernel,
         out_shape=jax.ShapeDtypeStruct((devices, groups * samples), jnp.bfloat16),
-        in_specs=[pl.BlockSpec(memory_space=pl.ANY)] + [vmem] * 5,
+        in_specs=[pl.BlockSpec(memory_space=pl.ANY)] * 6,
         out_specs=vmem,
         scratch_shapes=[
             pltpu.VMEM((comps, nodes, samples), jnp.bfloat16),
+            pltpu.VMEM((slots - 1, comps, slots - 1), jnp.bfloat16),
+            pltpu.VMEM(dip_taps.shape, jnp.bfloat16),
+            pltpu.VMEM((1, nodes), jnp.int32),
+            pltpu.VMEM((1, nodes), jnp.int32),
+            pltpu.VMEM((1, devices), jnp.int32),
             pltpu.VMEM((comps, nodes, slots * nodes), jnp.bfloat16),
             pltpu.VMEM((comps, slots * nodes, 2 * samples), jnp.bfloat16),
             pltpu.VMEM((slots * devices, groups * samples), jnp.bfloat16),
@@ -249,7 +267,7 @@
             pltpu.VMEM((2, devices, 1, samples), jnp.float32),
             pltpu.VMEM((devices, 1, samples), jnp.float32),
             pltpu.VMEM((devices, 1, samples), jnp.float32),
-            pltpu.SemaphoreType.DMA,
+            pltpu.SemaphoreType.DMA((6,)),
             pltpu.SemaphoreType.DMA,
             pltpu.SemaphoreType.DMA,
             pltpu.SemaphoreType.DMA((2,)),
@@ -257,9 +275,9 @@
             pltpu.SemaphoreType.DMA,
         ],
         compiler_params=pltpu.CompilerParams(
-            collective_id=0, has_side_effects=True, vmem_limit_bytes=48 * 1024 * 1024
+            collective_id=0, has_side_effects=True, vmem_limit_bytes=60 * 1024 * 1024
         ),
-    )(records, fan_taps, dip_taps, live_mask, node_place[None], shot_place[None])
+    )(records, fan_taps.transpose(1, 0, 2), dip_taps, live_mask, node_place[None], shot_place[None])
     return result.reshape(devices, comps, each, samples)
 
 

time: 13.2 us -> 13.5 us (1.023)
  Pallas kernels: 10.8 us -> 11.9 us
  local copies, waits for them, and re-layouts: 2.1 us -> 1.39 us
    unnamed x11 -> x0, local copies, waits for them, and re-layouts: 1.47 us -> none
    pallas_call x1, Pallas kernels: 10.8 us -> 11.9 us  [on_device(): pl.pallas_call(kernel, out_shape=jax.ShapeDtypeStruct((devices, groups *...]
    reshape x1, local copies, waits for them, and re-layouts: 0.63 us -> 1.39 us  [on_device(): return result.reshape(devices, comps, each, samples)]
where the time goes in v2:
time: 13.5 us; the launch traced here: 13.3 us
  Pallas kernels  11.9 us (88%)
  local copies, waits for them, and re-layouts  1.39 us (10%)
    pallas_call x1, Pallas kernels, on_device(): pl.pallas_call(kernel, out_shape=jax.ShapeDtypeStruct((devices, groups *...  11.9 us
    reshape x1, local copies, waits for them, and re-layouts, on_device(): return result.reshape(devices, comps, each, samples)  1.39 us

profile of v2, /device:TPU:0, one launch (start us, length us, event | category | flops | bytes accessed | tf_op | source)
XLA Modules:
  0.0 13.3 jit_solution(3483409101839190640)
XLA Ops:
  0.0 11.9 %shard_map.64 = bf16[16,1024]{1,0:T(8,128)(2,1)} custom-call(bf16[1,4,32,128]{3,2,1,0:T(8,128)(2,1)} %records_src.1, bf16[15,4,15]{2,1,0:T(4,128)(2,1)} %bitcast.3, bf16[15,15]{1,0:T(8,128)(2,1)} %dip_src.1, s32[1,32]{1,0:T(1,128)} %live_src.1, s32[1,32]{1,0:T(1,128)} %bitcast.4, s32[1,16]{1,0:T(1,128)} %bitcast.5), custom_call_target="tpu_custom_call" | custom-call | tf_op jit(solution)/shard_map/pallas_call | solution.py:248
  11.9 1.4 %reshape.3 = bf16[16,4,2,128]{3,2,1,0:T(2,128)(2,1)} reshape(bf16[16,1024]{1,0:T(8,128)(2,1)} %shard_map.64) | data formatting | bytes 65536 | tf_op jit(solution)/shard_map/reshape | solution.py:281

commit v3 on v1

--- a/solution.py
+++ b/solution.py
@@ -34,23 +34,20 @@
 
 
 def kernel(
-    records_ref, fan_ref, dip_ref, live_ref, node_ref, shot_ref, out_ref,
-    traces, matrix, shifted, framed, send, recv, flat, rows, pack, from_low, from_high,
-    load_sem, send_sem, recv_sem, pack_sem, low_sem, high_sem,
+    traces, taps_ref, live_ref, node_ref, shot_ref, out_ref,
+    matrix, shifted, framed, send, recv, flat, rows, pack, from_low, from_high,
+    send_sem, recv_sem, pack_sem, low_sem, high_sem,
 ):
-    comps, nodes, samples = traces.shape
+    _, comps, nodes, samples = traces.shape
     devices = send.shape[0]
     each = nodes // devices
     groups = comps * each
-    tap_count = dip_ref.shape[0]
+    tap_count = taps_ref.shape[1]
     reach = (tap_count - 1) // 2
     me, win = lax.axis_index("shot"), lax.axis_index("tm")
     windows = lax.axis_size("tm")
     has_low, has_high = win > 0, win < windows - 1
 
-    load = pltpu.make_async_copy(records_ref.at[0], traces, load_sem)
-    load.start()
-
     barrier = pltpu.get_barrier_semaphore()
 
     def greet(step):
@@ -68,7 +65,7 @@
             ))
 
     depth = matrix.shape[2]
-    taps = [spread_taps(fan_ref[c], nodes, depth) for c in range(comps)]
+    taps = [spread_taps(taps_ref[c], nodes, depth) for c in range(comps)]
     places = spread_places(node_ref[...], nodes, depth)[0:1]
     block = min(devices, 16)
 
@@ -98,19 +95,18 @@
         kept = jnp.where(here, live_ref[...].astype(jnp.float32), 0.0)
         alive.append(jnp.sum(kept, axis=1, keepdims=True))
 
-    load.wait()
     lane = lax.broadcasted_iota(jnp.int32, (nodes, samples), 1)
     for c in range(comps):
-        trace = traces[c].astype(jnp.float32)
+        trace = traces[0, c]
         for b in range(tap_count):
             move = b - reach
             turned = pltpu.roll(trace, (-move) % samples, 1) if move else trace
             inside = (lane < samples - move) if move >= 0 else (lane >= -move)
             shifted[c, b * nodes : (b + 1) * nodes, :samples] = (
-                jnp.where(inside, turned, 0.0).astype(jnp.bfloat16)
+                jnp.where(inside, turned, jnp.bfloat16(0))
             )
             shifted[c, b * nodes : (b + 1) * nodes, samples:] = (
-                jnp.where(inside, 0.0, turned).astype(jnp.bfloat16)
+                jnp.where(inside, jnp.bfloat16(0), turned)
             )
         rest = depth - tap_count * nodes
         shifted[c, tap_count * nodes :, :] = jnp.zeros((rest, 2 * samples), jnp.bfloat16)
@@ -170,7 +166,7 @@
     recv[me] = send[me]
 
     span = framed.shape[0]
-    dips = spread_taps(dip_ref[...], devices, span)
+    dips = spread_taps(taps_ref[comps], devices, span)
     apart = (
         spread_places(shot_ref[...], devices, span)[0:1]
         - lax.broadcasted_iota(jnp.int32, (devices, span), 0) + reach
@@ -205,6 +201,7 @@
         outer = rows[pl.ds(groups + g, devices, stride=2 * groups), :]
         inner = inner + jnp.where(tail, high, jnp.where(head, low, 0.0))
         outer = jnp.where(keep, outer + jnp.where(head, high, low), 0.0)
+        inner, outer = inner.astype(jnp.bfloat16), outer.astype(jnp.bfloat16)
         columns = slice(g * samples, (g + 1) * samples)
         for b in range(tap_count):
             move = b - reach
@@ -213,7 +210,7 @@
             else:
                 both = jnp.where(lane >= samples + move, outer, inner)
             turned = pltpu.roll(both, (-move) % samples, 1) if move else inner
-            framed[b * devices : (b + 1) * devices, columns] = turned.astype(jnp.bfloat16)
+            framed[b * devices : (b + 1) * devices, columns] = turned
     rest = span - tap_count * devices
     framed[tap_count * devices :, :] = jnp.zeros((rest, groups * samples), jnp.bfloat16)
     out_ref[...] = jnp.dot(dip, framed[...], preferred_element_type=jnp.float32).astype(jnp.bfloat16)
@@ -231,14 +228,14 @@
     each = nodes // devices
     groups = comps * each
     slots = fan_taps.shape[1] + 1
+    taps = jnp.concatenate([fan_taps, dip_taps[None]])
     vmem = pl.BlockSpec(memory_space=pltpu.VMEM)
     result = pl.pallas_call(
         kernel,
         out_shape=jax.ShapeDtypeStruct((devices, groups * samples), jnp.bfloat16),
-        in_specs=[pl.BlockSpec(memory_space=pl.ANY)] + [vmem] * 5,
+        in_specs=[vmem] * 5,
         out_specs=vmem,
         scratch_shapes=[
-            pltpu.VMEM((comps, nodes, samples), jnp.bfloat16),
             pltpu.VMEM((comps, nodes, slots * nodes), jnp.bfloat16),
             pltpu.VMEM((comps, slots * nodes, 2 * samples), jnp.bfloat16),
             pltpu.VMEM((slots * devices, groups * samples), jnp.bfloat16),
@@ -251,7 +248,6 @@
             pltpu.VMEM((devices, 1, samples), jnp.float32),
             pltpu.SemaphoreType.DMA,
             pltpu.SemaphoreType.DMA,
-            pltpu.SemaphoreType.DMA,
             pltpu.SemaphoreType.DMA((2,)),
             pltpu.SemaphoreType.DMA,
             pltpu.SemaphoreType.DMA,
@@ -259,7 +255,7 @@
         compiler_params=pltpu.CompilerParams(
             collective_id=0, has_side_effects=True, vmem_limit_bytes=48 * 1024 * 1024
         ),
-    )(records, fan_taps, dip_taps, live_mask, node_place[None], shot_place[None])
+    )(records, taps, live_mask, node_place[None], shot_place[None])
     return result.reshape(devices, comps, each, samples)
 
 

time: 13.2 us -> 13 us (0.985)
  no operation moved by 1% of the time
where the time goes in v3:
time: 13 us; the launch traced here: 12.7 us
  Pallas kernels  10.7 us (82%)
  local copies, waits for them, and re-layouts  2.02 us (16%)
    pallas_call x1, Pallas kernels, on_device(): pl.pallas_call(kernel, out_shape=jax.ShapeDtypeStruct((devices, groups *...  10.7 us
    unnamed x11, local copies, waits for them, and re-layouts  1.39 us
    reshape x1, local copies, waits for them, and re-layouts, on_device(): return result.reshape(devices, comps, each, samples)  0.63 us

profile of v3, /device:TPU:0, one launch (start us, length us, event | category | flops | bytes accessed | tf_op | source)
XLA Modules:
  0.0 12.7 jit_solution(8544334357141745672)
XLA Ops:
  0.0 0.0 copy-start.4
  0.0 0.0 copy-start
  0.0 0.7 %copy.7 = bf16[4,15,15]{2,1,0:T(8,128)(2,1)S(1)} copy(bf16[4,15,15]{2,0,1:T(4,128)(2,1)} %param.7) | data formatting | bytes 3600 | tf_op args[1]
  0.7 0.0 copy-done.4
  0.7 0.0 copy-start.1
  0.7 0.0 copy-start.2
  0.8 0.0 copy-start.3
  0.8 0.0 copy-done
  0.8 0.6 %copy-done.1 = s32[1,32]{1,0:T(1,128)S(1)} copy-done((s32[1,32]{1,0:T(1,128)S(1)}, s32[1,32]{1,0:T(1,128)}, u32[]{:S(2)}) %copy-start.1) | copy-done | bytes 152
  1.4 0.0 copy-done.2
  1.4 0.0 copy-done.3
  1.4 10.7 %shard_map.64 = bf16[16,1024]{1,0:T(8,128)(2,1)S(1)} custom-call(bf16[1,4,32,128]{3,2,1,0:T(8,128)(2,1)S(1)} %copy-done, bf16[5,15,15]{2,1,0:T(8,128)(2,1)S(1)} %pad_maximum_fusion.taps_ref, s32[1,32]{1,0:T(1,128)S(1)} %copy-done.1, s32[1,32]{1,0:T(1,128)S(1)} %bitcast.3, s32[1,16]{1,0:T(1,128)S(1)} %bitcast.4), custom_call_target="tpu_custom_call" | custom-call | tf_op jit(solution)/shard_map/pallas_call | solution.py:233
  12.1 0.6 %reshape.3 = bf16[16,4,2,128]{3,2,1,0:T(2,128)(2,1)} reshape(bf16[16,1024]{1,0:T(8,128)(2,1)S(1)} %shard_map.64) | data formatting | bytes 65536 | tf_op jit(solution)/shard_map/reshape | solution.py:259
  (1 shorter events, 0.0 us)
Async XLA Ops:
  0.0 0.7 %copy-start.4 = (bf16[15,15]{1,0:T(8,128)(2,1)S(1)}, bf16[15,15]{1,0:T(8,128)(2,1)}, u32[]{:S(2)}) copy-start(bf16[15,15]{1,0:T(8,128)(2,1)} %param.8) | copy-start | bytes 1354
  0.0 0.8 %copy-start = (bf16[1,4,32,128]{3,2,1,0:T(8,128)(2,1)S(1)}, bf16[1,4,32,128]{3,2,1,0:T(8,128)(2,1)}, u32[]{:S(2)}) copy-start(bf16[1,4,32,128]{3,2,1,0:T(8,128)(2,1)} %traces.1) | copy-start | bytes 98308
  0.7 0.7 %copy-start.1 = (s32[1,32]{1,0:T(1,128)S(1)}, s32[1,32]{1,0:T(1,128)}, u32[]{:S(2)}) copy-start(s32[1,32]{1,0:T(1,128)} %live_ref.1) | copy-start | bytes 388
  0.7 0.7 %copy-start.2 = (s32[32]{0:T(128)S(1)}, s32[32]{0:T(128)}, u32[]{:S(2)}) copy-start(s32[32]{0:T(128)} %param.10) | copy-start | bytes 388
  0.8 0.7 %copy-start.3 = (s32[16]{0:T(128)S(1)}, s32[16]{0:T(128)}, u32[]{:S(2)}) copy-start(s32[16]{0:T(128)} %param.11) | copy-start | bytes 196

commit v4 on v3

--- a/solution.py
+++ b/solution.py
@@ -16,6 +16,10 @@
             body(step)
     else:
         lax.fori_loop(0, count, lambda step, carry: (body(step), carry)[1], 0)
+
+
+def far_first(step, count):
+    return count // 2 + (1 - 2 * (step % 2)) * ((step + 1) // 2)
 
 
 def spread_taps(taps, groups, width):
@@ -52,7 +56,7 @@
 
     def greet(step):
         pl.semaphore_signal(
-            barrier, inc=1, device_id=(lax.rem(me + step + 1, devices), win), device_id_type=MESH
+            barrier, inc=1, device_id=(lax.rem(me + far_first(step, devices), devices), win), device_id_type=MESH
         )
 
     repeat(devices - 1, greet)
@@ -60,7 +64,7 @@
         @pl.when(there)
         def _():
             repeat(devices, lambda step: pl.semaphore_signal(
-                barrier, inc=1, device_id=(lax.rem(me + step, devices), win + side),
+                barrier, inc=1, device_id=(lax.rem(me + far_first(step, devices), devices), win + side),
                 device_id_type=MESH,
             ))
 
@@ -139,13 +143,12 @@
     )
 
     def post(step):
-        target = lax.rem(me + step + 1, devices)
+        target = lax.rem(me + far_first(step, devices), devices)
         pltpu.make_async_remote_copy(
             src_ref=send.at[target], dst_ref=recv.at[me], send_sem=send_sem, recv_sem=recv_sem,
             device_id=(target, win), device_id_type=MESH,
         ).start()
 
-    repeat(devices - 1, post)
     sides = (
         (has_low, -1, 0, from_high, high_sem),
         (has_high, 1, 1, from_low, low_sem),
@@ -154,7 +157,7 @@
         @pl.when(there)
         def _():
             def post_side(step):
-                target = lax.rem(me + step, devices)
+                target = lax.rem(me + far_first(step, devices), devices)
                 pltpu.make_async_remote_copy(
                     src_ref=pack.at[slot, target], dst_ref=landing.at[me],
                     send_sem=pack_sem.at[slot], recv_sem=landed,
@@ -163,6 +166,7 @@
 
             repeat(devices, post_side)
 
+    repeat(devices - 1, post)
     recv[me] = send[me]
 
     span = framed.shape[0]

time: 13 us -> 12.9 us (level)
  Pallas kernels: 10.7 us -> 10.5 us
where the time goes in v4:
time: 12.9 us; the launch traced here: 12.6 us
  Pallas kernels  10.5 us (81%)
  local copies, waits for them, and re-layouts  2.02 us (16%)
    pallas_call x1, Pallas kernels, on_device(): pl.pallas_call(kernel, out_shape=jax.ShapeDtypeStruct((devices, groups *...  10.5 us
    unnamed x11, local copies, waits for them, and re-layouts  1.39 us
    reshape x1, local copies, waits for them, and re-layouts, on_device(): return result.reshape(devices, comps, each, samples)  0.63 us

profile of v4, /device:TPU:0, one launch (start us, length us, event | category | flops | bytes accessed | tf_op | source)
XLA Modules:
  0.0 12.6 jit_solution(3534611702275523484)
XLA Ops:
  0.0 0.0 copy-start.4
  0.0 0.0 copy-start
  0.0 0.7 %copy.7 = bf16[4,15,15]{2,1,0:T(8,128)(2,1)S(1)} copy(bf16[4,15,15]{2,0,1:T(4,128)(2,1)} %param.7) | data formatting | bytes 3600 | tf_op args[1]
  0.7 0.0 copy-done.4
  0.7 0.0 copy-start.1
  0.7 0.0 copy-start.2
  0.8 0.0 copy-start.3
  0.8 0.0 copy-done
  0.8 0.6 %copy-done.1 = s32[1,32]{1,0:T(1,128)S(1)} copy-done((s32[1,32]{1,0:T(1,128)S(1)}, s32[1,32]{1,0:T(1,128)}, u32[]{:S(2)}) %copy-start.1) | copy-done | bytes 152
  1.4 0.0 copy-done.2
  1.4 0.0 copy-done.3
  1.4 10.5 %shard_map.64 = bf16[16,1024]{1,0:T(8,128)(2,1)S(1)} custom-call(bf16[1,4,32,128]{3,2,1,0:T(8,128)(2,1)S(1)} %copy-done, bf16[5,15,15]{2,1,0:T(8,128)(2,1)S(1)} %pad_maximum_fusion.taps_ref, s32[1,32]{1,0:T(1,128)S(1)} %copy-done.1, s32[1,32]{1,0:T(1,128)S(1)} %bitcast.3, s32[1,16]{1,0:T(1,128)S(1)} %bitcast.4), custom_call_target="tpu_custom_call" | custom-call | tf_op jit(solution)/shard_map/pallas_call | solution.py:237
  12.0 0.6 %reshape.3 = bf16[16,4,2,128]{3,2,1,0:T(2,128)(2,1)} reshape(bf16[16,1024]{1,0:T(8,128)(2,1)S(1)} %shard_map.64) | data formatting | bytes 65536 | tf_op jit(solution)/shard_map/reshape | solution.py:263
  (1 shorter events, 0.0 us)
Async XLA Ops:
  0.0 0.7 %copy-start.4 = (bf16[15,15]{1,0:T(8,128)(2,1)S(1)}, bf16[15,15]{1,0:T(8,128)(2,1)}, u32[]{:S(2)}) copy-start(bf16[15,15]{1,0:T(8,128)(2,1)} %param.8) | copy-start | bytes 1354
  0.0 0.8 %copy-start = (bf16[1,4,32,128]{3,2,1,0:T(8,128)(2,1)S(1)}, bf16[1,4,32,128]{3,2,1,0:T(8,128)(2,1)}, u32[]{:S(2)}) copy-start(bf16[1,4,32,128]{3,2,1,0:T(8,128)(2,1)} %traces.1) | copy-start | bytes 98308
  0.7 0.7 %copy-start.1 = (s32[1,32]{1,0:T(1,128)S(1)}, s32[1,32]{1,0:T(1,128)}, u32[]{:S(2)}) copy-start(s32[1,32]{1,0:T(1,128)} %live_ref.1) | copy-start | bytes 388
  0.7 0.7 %copy-start.2 = (s32[32]{0:T(128)S(1)}, s32[32]{0:T(128)}, u32[]{:S(2)}) copy-start(s32[32]{0:T(128)} %param.10) | copy-start | bytes 388
  0.8 0.7 %copy-start.3 = (s32[16]{0:T(128)S(1)}, s32[16]{0:T(128)}, u32[]{:S(2)}) copy-start(s32[16]{0:T(128)} %param.11) | copy-start | bytes 196

commit v5 on v4

--- a/solution.py
+++ b/solution.py
@@ -179,6 +179,9 @@
     for a in range(tap_count):
         dip = jnp.where(apart == a, dips[a : a + 1], dip)
     dip = dip.astype(jnp.bfloat16)
+
+    rest = span - tap_count * devices
+    framed[tap_count * devices :, :] = jnp.zeros((rest, groups * samples), jnp.bfloat16)
 
     for there, landing, landed in ((has_high, from_high, high_sem), (has_low, from_low, low_sem)):
         @pl.when(there)
@@ -215,9 +218,11 @@
                 both = jnp.where(lane >= samples + move, outer, inner)
             turned = pltpu.roll(both, (-move) % samples, 1) if move else inner
             framed[b * devices : (b + 1) * devices, columns] = turned
-    rest = span - tap_count * devices
-    framed[tap_count * devices :, :] = jnp.zeros((rest, groups * samples), jnp.bfloat16)
-    out_ref[...] = jnp.dot(dip, framed[...], preferred_element_type=jnp.float32).astype(jnp.bfloat16)
+        if g % 2 == 1 or g == groups - 1:
+            columns = slice(g // 2 * 2 * samples, (g + 1) * samples)
+            out_ref[:, columns] = jnp.dot(
+                dip, framed[:, columns], preferred_element_type=jnp.float32
+            ).astype(jnp.bfloat16)
 
     sent = send.at[pl.ds(0, devices - 1)]
     pltpu.make_async_copy(sent, sent, send_sem).wait()

time: 12.9 us -> 12.9 us (level)
  no operation moved by 1% of the time
where the time goes in v5:
time: 12.9 us; the launch traced here: 12.6 us
  Pallas kernels  10.5 us (81%)
  local copies, waits for them, and re-layouts  2.02 us (16%)
    pallas_call x1, Pallas kernels, on_device(): pl.pallas_call(kernel, out_shape=jax.ShapeDtypeStruct((devices, groups *...  10.5 us
    unnamed x11, local copies, waits for them, and re-layouts  1.39 us
    reshape x1, local copies, waits for them, and re-layouts, on_device(): return result.reshape(devices, comps, each, samples)  0.63 us

profile of v5, /device:TPU:0, one launch (start us, length us, event | category | flops | bytes accessed | tf_op | source)
XLA Modules:
  0.0 12.6 jit_solution(8182412883739811147)
XLA Ops:
  0.0 0.0 copy-start.4
  0.0 0.0 copy-start
  0.0 0.7 %copy.7 = bf16[4,15,15]{2,1,0:T(8,128)(2,1)S(1)} copy(bf16[4,15,15]{2,0,1:T(4,128)(2,1)} %param.7) | data formatting | bytes 3600 | tf_op args[1]
  0.7 0.0 copy-done.4
  0.7 0.0 copy-start.1
  0.7 0.0 copy-start.2
  0.8 0.0 copy-start.3
  0.8 0.0 copy-done
  0.8 0.6 %copy-done.1 = s32[1,32]{1,0:T(1,128)S(1)} copy-done((s32[1,32]{1,0:T(1,128)S(1)}, s32[1,32]{1,0:T(1,128)}, u32[]{:S(2)}) %copy-start.1) | copy-done | bytes 152
  1.4 0.0 copy-done.2
  1.4 0.0 copy-done.3
  1.4 10.5 %shard_map.64 = bf16[16,1024]{1,0:T(8,128)(2,1)S(1)} custom-call(bf16[1,4,32,128]{3,2,1,0:T(8,128)(2,1)S(1)} %copy-done, bf16[5,15,15]{2,1,0:T(8,128)(2,1)S(1)} %pad_maximum_fusion.taps_ref, s32[1,32]{1,0:T(1,128)S(1)} %copy-done.1, s32[1,32]{1,0:T(1,128)S(1)} %bitcast.3, s32[1,16]{1,0:T(1,128)S(1)} %bitcast.4), custom_call_target="tpu_custom_call" | custom-call | tf_op jit(solution)/shard_map/pallas_call | solution.py:242
  12.0 0.6 %reshape.3 = bf16[16,4,2,128]{3,2,1,0:T(2,128)(2,1)} reshape(bf16[16,1024]{1,0:T(8,128)(2,1)S(1)} %shard_map.64) | data formatting | bytes 65536 | tf_op jit(solution)/shard_map/reshape | solution.py:268
  (1 shorter events, 0.0 us)
Async XLA Ops:
  0.0 0.7 %copy-start.4 = (bf16[15,15]{1,0:T(8,128)(2,1)S(1)}, bf16[15,15]{1,0:T(8,128)(2,1)}, u32[]{:S(2)}) copy-start(bf16[15,15]{1,0:T(8,128)(2,1)} %param.8) | copy-start | bytes 1354
  0.0 0.8 %copy-start = (bf16[1,4,32,128]{3,2,1,0:T(8,128)(2,1)S(1)}, bf16[1,4,32,128]{3,2,1,0:T(8,128)(2,1)}, u32[]{:S(2)}) copy-start(bf16[1,4,32,128]{3,2,1,0:T(8,128)(2,1)} %traces.1) | copy-start | bytes 98308
  0.7 0.7 %copy-start.1 = (s32[1,32]{1,0:T(1,128)S(1)}, s32[1,32]{1,0:T(1,128)}, u32[]{:S(2)}) copy-start(s32[1,32]{1,0:T(1,128)} %live_ref.1) | copy-start | bytes 388
  0.7 0.7 %copy-start.2 = (s32[32]{0:T(128)S(1)}, s32[32]{0:T(128)}, u32[]{:S(2)}) copy-start(s32[32]{0:T(128)} %param.10) | copy-start | bytes 388
  0.8 0.7 %copy-start.3 = (s32[16]{0:T(128)S(1)}, s32[16]{0:T(128)}, u32[]{:S(2)}) copy-start(s32[16]{0:T(128)} %param.11) | copy-start | bytes 196
